TPU v7x, 256 devices: a whole 4x4x8 slice. The times are simulated.
256 devices in a mesh: shard: 32 (over x, z_lo, core), rep: 8 (over z_hi, y).
Axes of the slice: x: 4, y: 4, z: 8 (z_hi: 2, z_lo: 4; z = z_hi * 4 + z_lo), core: 2. Of those that a mesh axis runs over, the one named last changes fastest.
Arguments:
- queries: bfloat16 [8, 4096, 2048], P('rep', 'shard'), may hold values from -20 to 20
- key_vectors: bfloat16 [8, 4096, 2048], P('rep', 'shard'), may hold values from -7.5 to 7.5
- value_vectors: bfloat16 [8, 4096, 2048], P('rep', 'shard'), may hold values from -6 to 6
- neighbor_ids: int32 [8, 32, 2], P('rep', 'shard'), may hold values from 0 to 31, as said below
- upstream: bfloat16 [8, 4096, 2048], P('rep', 'shard'), may hold values from -6 to 6
- w_out: bfloat16 [2048, 2048], P('shard'), may hold values from -0.125 to 0.125
Outputs:
- projected: bfloat16 [8, 4096, 2048], P('rep', 'shard')
- grad_queries: bfloat16 [8, 4096, 2048], P('rep', 'shard')
- grad_keys: bfloat16 [8, 4096, 2048], P('rep', 'shard')
- grad_values: bfloat16 [8, 4096, 2048], P('rep', 'shard')
- grad_w_out: float32 [2048, 2048], P('shard')
Inputs may be any that keep to these rules, and one draw needn't show every extreme that they name: neighbor_ids[m, p, 0] is p - 1 if patch p is linked to patch p - 1 and p otherwise; neighbor_ids[m, p, 1] is p + 1 if patch p is linked to patch p + 1 and p otherwise; links are symmetric; patch 0 has no link before it and patch 32 - 1 none after it; patches p and p + 1 are linked whenever p is even.
All inputs are finite; a program needn't handle non-finite values.
Results may differ from a plain program's by a relative error of at most 0.009.
Values may be sent and summed in bfloat16 or wider, within the bound.
A program may use at most 128 MiB of HBM per device.

v0:
```python
import jax
import jax.numpy as jnp
from jax import lax
from jax.sharding import PartitionSpec as P

HEADS = 16
DH = 128
PATCH = 128


def extended_2(block, sides, width):
    for axis, dim in sides:
        count = lax.axis_size(axis)
        forward = [(i, i + 1) for i in range(count - 1)]
        backward = [(target, source) for source, target in forward]
        low = lax.ppermute(
            lax.slice_in_dim(block, block.shape[dim] - width, None, axis=dim), axis, forward
        )
        high = lax.ppermute(lax.slice_in_dim(block, 0, width, axis=dim), axis, backward)
        block = jnp.concatenate([low, block, high], axis=dim)
    return block


def shifted(value, axis, steps):
    count = lax.axis_size(axis)
    initial, last = (max(0, -steps), min(count, count - steps))
    return lax.ppermute(value, axis, [(source, source + steps) for source in range(initial, last)])


def windows_of(extended, local_count):
    blocks = extended.reshape(local_count + 2, PATCH, HEADS, DH)
    return jnp.concatenate([blocks[:-2], blocks[1:-1], blocks[2:]], axis=1)


def spread_terms(terms, local_count):
    widened = terms.astype(jnp.float32).reshape(local_count, 3, PATCH, HEADS * DH)
    edges = ((0, 0), (0, 0))
    return (
        jnp.pad(widened[:, 0], ((0, 2),) + edges)
        + jnp.pad(widened[:, 1], ((1, 1),) + edges)
        + jnp.pad(widened[:, 2], ((2, 0),) + edges)
    )


def per_device(queries, key_vectors, value_vectors, neighbor_ids, upstream, w_out):
    query_rows = queries[0]
    key_rows = key_vectors[0]
    value_rows = value_vectors[0]
    link_ids = neighbor_ids[0]
    upstream_rows = upstream[0]
    node_count = query_rows.shape[0]
    local_count = node_count // PATCH
    hidden_width = query_rows.shape[1]
    scaling = DH ** (-0.5)
    grad_factor = float(node_count * lax.axis_size("shard") * lax.axis_size("rep")) ** (-0.5)
    patch_ids = lax.axis_index("shard") * local_count + jnp.arange(local_count, dtype=jnp.int32)
    left_ok = link_ids[:, 0] != patch_ids
    right_ok = link_ids[:, 1] != patch_ids
    allowed = jnp.concatenate(
        [
            jnp.broadcast_to(left_ok[:, None], (local_count, PATCH)),
            jnp.ones((local_count, PATCH), jnp.bool_),
            jnp.broadcast_to(right_ok[:, None], (local_count, PATCH)),
        ],
        axis=1,
    )
    key_ext, value_ext = (
        extended_2(key_rows, (("shard", 0),), PATCH),
        extended_2(value_rows, (("shard", 0),), PATCH),
    )
    key_win = windows_of(key_ext, local_count)
    value_win = windows_of(value_ext, local_count)
    query_blk = query_rows.reshape(local_count, PATCH, HEADS, DH)
    scores = (
        jnp.einsum("pqhd,pkhd->phqk", query_blk, key_win, preferred_element_type=jnp.float32)
        * scaling
    )
    key_mask = allowed[:, None, None, :]
    highest = jnp.max(jnp.where(key_mask, scores, -jnp.inf), axis=-1)
    numerators = jnp.where(key_mask, jnp.exp(scores - highest[..., None]), 0.0)
    totals = jnp.sum(numerators, axis=-1)
    probabilities = numerators / totals[..., None]
    prob_half = probabilities.astype(jnp.bfloat16)
    attended = jnp.einsum(
        "phqk,pkhd->pqhd", prob_half, value_win, preferred_element_type=jnp.float32
    )
    attended = attended.astype(jnp.bfloat16).reshape(node_count, hidden_width)
    shard_rows = lax.all_gather(w_out, "shard", axis=0, tiled=True)
    columns = attended
    out_total = jnp.dot(columns, shard_rows, preferred_element_type=jnp.float32)
    product = lax.dot_general(
        upstream_rows, shard_rows, (((1,), (1,)), ((), ())), preferred_element_type=jnp.float32
    )
    grad_total = product
    out_total, grad_total = (out_total, grad_total)
    projected = out_total.astype(jnp.bfloat16)
    grad_attended = grad_total.astype(jnp.bfloat16)
    grad_blk = grad_attended.reshape(local_count, PATCH, HEADS, DH)
    prob_grad = jnp.einsum(
        "pqhd,pkhd->phqk", grad_blk, value_win, preferred_element_type=jnp.float32
    )
    row_delta = jnp.sum(probabilities * prob_grad, axis=-1)
    score_grad = (probabilities * (prob_grad - row_delta[..., None])).astype(jnp.bfloat16)
    grad_queries = (
        jnp.einsum("phqk,pkhd->pqhd", score_grad, key_win, preferred_element_type=jnp.float32)
        * scaling
    )
    grad_queries = grad_queries.astype(jnp.bfloat16).reshape(node_count, hidden_width)
    key_terms = (
        jnp.einsum("phqk,pqhd->pkhd", score_grad, query_blk, preferred_element_type=jnp.float32)
        * scaling
    ).astype(jnp.bfloat16)
    value_terms = jnp.einsum(
        "phqk,pqhd->pkhd", prob_half, grad_blk, preferred_element_type=jnp.float32
    ).astype(jnp.bfloat16)
    key_sums = spread_terms(key_terms, local_count)
    value_sums = spread_terms(value_terms, local_count)
    from_upper = shifted(
        (key_sums[0].astype(jnp.bfloat16), value_sums[0].astype(jnp.bfloat16)), "shard", -1
    )
    from_lower = shifted(
        (
            key_sums[local_count + 1].astype(jnp.bfloat16),
            value_sums[local_count + 1].astype(jnp.bfloat16),
        ),
        "shard",
        1,
    )
    inner_keys = key_sums[1 : local_count + 1]
    inner_keys = (
        inner_keys.at[0]
        .add(from_lower[0].astype(jnp.float32))
        .at[local_count - 1]
        .add(from_upper[0].astype(jnp.float32))
    )
    inner_values = value_sums[1 : local_count + 1]
    inner_values = (
        inner_values.at[0]
        .add(from_lower[1].astype(jnp.float32))
        .at[local_count - 1]
        .add(from_upper[1].astype(jnp.float32))
    )
    grad_keys = inner_keys.astype(jnp.bfloat16).reshape(node_count, hidden_width)
    grad_values = inner_values.astype(jnp.bfloat16).reshape(node_count, hidden_width)
    columns = attended
    product = lax.dot_general(
        columns, upstream_rows, (((0,), (0,)), ((), ())), preferred_element_type=jnp.float32
    )
    shard_sum = lax.psum_scatter(product * grad_factor, "shard", scatter_dimension=0, tiled=True)
    grad_w_out = lax.psum(shard_sum, "rep")
    return (projected[None], grad_queries[None], grad_keys[None], grad_values[None], grad_w_out)


def solution(mesh):
    placed = (
        P("rep", "shard", None),
        P("rep", "shard", None),
        P("rep", "shard", None),
        P("rep", "shard", None),
        P("rep", "shard", None),
        P("shard", None),
    )
    return jax.shard_map(
        per_device,
        mesh=mesh,
        in_specs=placed,
        out_specs=(
            P("rep", "shard", None),
            P("rep", "shard", None),
            P("rep", "shard", None),
            P("rep", "shard", None),
            P("shard", None),
        ),
        check_vma=False,
    )
```

profile of v0, /device:TPU:90, one launch (start us, length us, event | category | flops | bytes accessed | tf_op | source)
XLA Modules:
  0.0 421.0 jit_solution(10076020013242272677)
XLA Ops:
  11.2 2.4 collective-permute-start.2
  13.6 3.2 collective-permute-start.1
  16.8 2.2 collective-permute-start
  24.8 7.2 %collective-permute-done.2 = bf16[128,2048]{0,1:T(8,128)(2,1)} collective-permute-done((bf16[128,2048]{0,1:T(8,128)(2,1)S(1)}, bf16[128,2048]{0,1:T(8,128)(2,1)}, u32[]{:S(2)}, u32[]{:S(2)}) %collective-permute-start.2) | collective-permute-done | bytes 524320 | tf_op jit(solution)/shard_map/ppermute | solution.py:16
  33.4 6.3 %collective-permute-done.1 = bf16[128,2048]{1,0:T(8,128)(2,1)} collective-permute-done((bf16[128,2048]{1,0:T(8,128)(2,1)}, bf16[128,2048]{1,0:T(8,128)(2,1)}, u32[]{:S(2)}, u32[]{:S(2)}) %collective-permute-start.1) | collective-permute-done | bytes 524320 | tf_op jit(solution)/shard_map/ppermute | solution.py:19
  41.7 9.9 %collective-permute-done = bf16[128,2048]{1,0:T(8,128)(2,1)} collective-permute-done((bf16[128,2048]{1,0:T(8,128)(2,1)}, bf16[128,2048]{1,0:T(8,128)(2,1)}, u32[]{:S(2)}, u32[]{:S(2)}) %collective-permute-start) | collective-permute-done | bytes 524320 | tf_op jit(solution)/shard_map/ppermute | solution.py:16
  57.0 8.1 %convolution_multiply_fusion = f32[2048,2048]{1,0:T(8,128)} fusion(bf16[128,2048]{0,1:T(8,128)(2,1)S(1)} %bitcast.119, bf16[1,128,2048]{2,1,0:T(8,128)(2,1)S(1)} %copy-done), kind=kOutput, calls=%fused_computation.1 | convolution fusion | flops 1077936128 | bytes 17825792 | tf_op jit(solution)/shard_map/dot_general | solution.py:146
  65.4 24.9 %all-gather.2.cloned.1.call-done = bf16[2048,2048]{1,0:T(8,128)(2,1)} async-done(((bf16[64,2048]{1,0:T(8,128)(2,1)}), bf16[2048,2048]{1,0:T(8,128)(2,1)}) %all-gather.2.cloned.1.call-update) | async-done | bytes 8388624 | tf_op jit(solution)/shard_map/all_gather | solution.py:88
  90.4 6.3 %convolution_convert_fusion = bf16[128,2048]{1,0:T(8,128)(2,1)S(1)} fusion(bf16[2048,2048]{1,0:T(8,128)(2,1)} %all-gather.2.cloned.1.call-done, bf16[1,128,2048]{2,1,0:T(8,128)(2,1)S(1)} %copy-done), kind=kOutput, calls=%fused_computation.15 | convolution fusion | flops 1074003968 | bytes 9437184 | tf_op jit(solution)/shard_map/dot_general | solution.py:91
  97.7 4.3 %convert_bitcast_fusion = f32[1,384,16,128]{1,3,2,0:T(8,128)} fusion(bf16[128,16,128]{0,2,1:T(8,128)(2,1)S(1)} %bitcast.136, f32[16,384,128]{2,1,0:T(8,128)} %copy-done.3, f32[16,128]{1,0:T(8,128)S(1)} %get-tuple-element.79), kind=kOutput, calls=%fused_computation.4 | convolution fusion | flops 204472320 | bytes 6823936 | tf_op jit(solution)/shard_map/phqk,pqhd->pkhd/dot_general | solution.py:113
  102.0 3.7 copy.51
  105.7 2.9 multiply_reduce_fusion
  111.7 2.2 slice_bitcast_fusion.5
  113.9 4.3 %fusion.29 = (bf16[3,128,2048]{2,0,1:T(4,128)(2,1)S(1)}, f32[3,128,2048]{2,0,1:T(4,128)}) fusion(f32[1,128,2048]{2,0,1:T(1,128)S(1)} %get-tuple-element.71, f32[1,128,2048]{2,0,1:T(1,128)S(1)} %get-tuple-element.72, f32[1,128,2048]{2,0,1:T(1,128)S(1)} %get-tuple-element.70), kind=kLoop, calls=%fused_computation.60 | loop fusion | flops 2359296 | bytes 7864320 | tf_op jit(solution)/shard_map/convert.13
  121.1 2.5 collective-permute-start.5
  125.8 2.2 slice_bitcast_fusion.2
  128.0 4.3 %fusion.30 = (bf16[3,128,2048]{2,0,1:T(4,128)(2,1)S(1)}, f32[3,128,2048]{2,0,1:T(4,128)}) fusion(f32[1,128,2048]{2,0,1:T(1,128)S(1)} %get-tuple-element.66, f32[1,128,2048]{2,0,1:T(1,128)S(1)} %get-tuple-element.67, f32[1,128,2048]{2,0,1:T(1,128)S(1)} %get-tuple-element.65), kind=kLoop, calls=%fused_computation.61 | loop fusion | flops 2359296 | bytes 7864320 | tf_op jit(solution)/shard_map/convert.11
  136.1 3.6 collective-permute-start.7
  145.6 3.3 slice.169
  148.9 3.3 slice.175
  152.2 150.4 %reduce-scatter.2.cloned.1.call-done = f32[64,2048]{1,0:T(8,128)} async-done(((f32[2048,2048]{1,0:T(8,128)}), f32[64,2048]{1,0:T(8,128)}) %reduce-scatter.2.cloned.1.call-update) | async-done | bytes 524304 | tf_op jit(solution)/shard_map/reduce_scatter | solution.py:149
  302.7 2.5 fusion.13
  305.2 2.5 fusion.11
  307.6 104.9 %all-reduce.8.cloned.1.call-done = f32[64,2048]{1,0:T(8,128)} async-done(((f32[64,2048]{1,0:T(8,128)}), f32[64,2048]{1,0:T(8,128)}) %all-reduce.8.cloned.1.call-update) | async-done | bytes 524304 | tf_op jit(solution)/shard_map/psum | solution.py:150
  (82 shorter events, 37.9 us)
Async XLA Ops:
  7.2 49.9 %copy-start = (bf16[1,128,2048]{2,1,0:T(8,128)(2,1)S(1)}, bf16[1,128,2048]{2,1,0:T(8,128)(2,1)}, u32[]{:S(2)}) copy-start(bf16[1,128,2048]{2,1,0:T(8,128)(2,1)} %param.18) | copy-start | bytes 1572868
  7.2 16.1 %copy-start.5 = (bf16[1,128,2048]{2,1,0:T(8,128)(2,1)S(1)}, bf16[1,128,2048]{2,1,0:T(8,128)(2,1)}, u32[]{:S(2)}) copy-start(bf16[1,128,2048]{2,1,0:T(8,128)(2,1)} %param.14) | copy-start | bytes 1572868
  7.2 83.2 %all-gather.2.cloned.1.call-start = ((), (), s32[]{:S(2)}) async-start(), calls=%async_computation.1 | async-start | bytes 8650752 | tf_op jit(solution)/shard_map/all_gather | solution.py:88
  7.9 294.7 %reduce-scatter.2.cloned.1.call-start = ((), (), s32[]{:S(2)}) async-start(), calls=%async_computation.2 | async-start | bytes 17301504 | tf_op jit(solution)/shard_map/reduce_scatter | solution.py:149
  9.3 14.2 %collective-permute-start.3 = (bf16[128,2048]{0,1:T(8,128)(2,1)S(1)}, bf16[128,2048]{0,1:T(8,128)(2,1)}, u32[]{:S(2)}, u32[]{:S(2)}) collective-permute-start(bf16[128,2048]{0,1:T(8,128)(2,1)S(1)} %bitcast.123), channel_id=1, source_target_pairs={{8,0},{16,8},{24,16},{32,24},{40,32},{48,40},{56,48},{64,56},{72,6... | collective-permute-start | bytes 1572872 | tf_op jit(solution)/shard_map/ppermute | solution.py:19
  11.2 20.8 %collective-permute-start.2 = (bf16[128,2048]{0,1:T(8,128)(2,1)S(1)}, bf16[128,2048]{0,1:T(8,128)(2,1)}, u32[]{:S(2)}, u32[]{:S(2)}) collective-permute-start(bf16[128,2048]{0,1:T(8,128)(2,1)S(1)} %bitcast.124), channel_id=1, source_target_pairs={{0,8},{8,16},{16,24},{24,32},{32,40},{40,48},{48,56},{56,64},{64,7... | collective-permute-start | bytes 1572872 | tf_op jit(solution)/shard_map/ppermute | solution.py:16
  13.6 26.0 %collective-permute-start.1 = (bf16[128,2048]{1,0:T(8,128)(2,1)}, bf16[128,2048]{1,0:T(8,128)(2,1)}, u32[]{:S(2)}, u32[]{:S(2)}) collective-permute-start(bf16[128,2048]{1,0:T(8,128)(2,1)} %bitcast.128), channel_id=1, source_target_pairs={{8,0},{16,8},{24,16},{32,24},{40,32},{48,40},{56,48},{64,56},{72,6... | collective-permute-start | bytes 1572872 | tf_op jit(solution)/shard_map/ppermute | solution.py:19
  16.8 34.8 %collective-permute-start = (bf16[128,2048]{1,0:T(8,128)(2,1)}, bf16[128,2048]{1,0:T(8,128)(2,1)}, u32[]{:S(2)}, u32[]{:S(2)}) collective-permute-start(bf16[128,2048]{1,0:T(8,128)(2,1)} %bitcast.129), channel_id=1, source_target_pairs={{0,8},{8,16},{16,24},{24,32},{32,40},{40,48},{48,56},{56,64},{64,7... | collective-permute-start | bytes 1572872 | tf_op jit(solution)/shard_map/ppermute | solution.py:16
  24.8 29.4 %copy-start.6 = (bf16[1,128,16,128]{3,1,2,0:T(8,128)(2,1)}, bf16[1,128,16,128]{3,1,2,0:T(8,128)(2,1)S(1)}, u32[]{:S(2)}) copy-start(bf16[1,128,16,128]{3,1,2,0:T(8,128)(2,1)S(1)} %copy.36) | copy-start | bytes 1572868
  33.4 20.9 %copy-start.8 = (bf16[1,128,16,128]{3,1,2,0:T(8,128)(2,1)}, bf16[1,128,16,128]{3,1,2,0:T(8,128)(2,1)S(1)}, u32[]{:S(2)}) copy-start(bf16[1,128,16,128]{3,1,2,0:T(8,128)(2,1)S(1)} %copy.34) | copy-start | bytes 1572868
  65.2 347.4 %all-reduce.8.cloned.1.call-start = ((), (), s32[]{:S(2)}) async-start(), calls=%async_computation.3 | async-start | bytes 1048576 | tf_op jit(solution)/shard_map/psum | solution.py:150
  102.0 3.7 copy-start.11
  102.0 3.7 copy-start.13
  105.7 3.0 copy-start.4
  118.2 7.5 %copy-start.2 = (f32[1,384,16,128]{3,2,0,1:T(8,128)S(1)}, f32[1,384,16,128]{3,2,0,1:T(8,128)}, u32[]{:S(2)}) copy-start(f32[1,384,16,128]{3,2,0,1:T(8,128)} %copy.51) | copy-start | bytes 9437188
  121.1 181.5 %collective-permute-start.5 = (bf16[128,2048]{1,0:T(8,128)(2,1)}, bf16[128,2048]{1,0:T(8,128)(2,1)}, u32[]{:S(2)}, u32[]{:S(2)}) collective-permute-start(bf16[128,2048]{1,0:T(8,128)(2,1)} %bitcast.114), channel_id=1, source_target_pairs={{8,0},{16,8},{24,16},{32,24},{40,32},{48,40},{56,48},{64,56},{72,6... | collective-permute-start | bytes 1572872 | tf_op jit(solution)/shard_map/ppermute | solution.py:27
  123.6 179.0 %collective-permute-start.4 = (bf16[128,2048]{1,0:T(8,128)(2,1)S(1)}, bf16[128,2048]{1,0:T(8,128)(2,1)}, u32[]{:S(2)}, u32[]{:S(2)}) collective-permute-start(bf16[128,2048]{1,0:T(8,128)(2,1)S(1)} %bitcast.126), channel_id=1, source_target_pairs={{0,8},{8,16},{16,24},{24,32},{32,40},{40,48},{48,56},{56,64},{64,7... | collective-permute-start | bytes 1572872 | tf_op jit(solution)/shard_map/ppermute | solution.py:27
  125.8 16.0 %slice-start = ((s8[8388608]{0:T(1024)(128)(4,1)}), s8[4194304]{0:T(1024)(128)(4,1)S(1)}, s32[]{:S(2)}) async-start(s8[8388608]{0:T(1024)(128)(4,1)} %bitcast.115), calls=%async_computation.4 | async-start | bytes 8388608
  128.0 13.8 %slice-start.1 = ((s8[8388608]{0:T(1024)(128)(4,1)}), s8[4194304]{0:T(1024)(128)(4,1)S(1)}, s32[]{:S(2)}) async-start(s8[8388608]{0:T(1024)(128)(4,1)} %bitcast.115), calls=%async_computation.5 | async-start | bytes 8388608
  136.1 169.1 %collective-permute-start.7 = (bf16[128,2048]{1,0:T(8,128)(2,1)}, bf16[128,2048]{1,0:T(8,128)(2,1)}, u32[]{:S(2)}, u32[]{:S(2)}) collective-permute-start(bf16[128,2048]{1,0:T(8,128)(2,1)} %bitcast.113), channel_id=1, source_target_pairs={{8,0},{16,8},{24,16},{32,24},{40,32},{48,40},{56,48},{64,56},{72,6... | collective-permute-start | bytes 1572872 | tf_op jit(solution)/shard_map/ppermute | solution.py:27
  139.7 4.2 copy-start.7
  139.7 4.2 copy-start.9
  139.7 165.4 %collective-permute-start.6 = (bf16[128,2048]{1,0:T(8,128)(2,1)}, bf16[128,2048]{1,0:T(8,128)(2,1)}, u32[]{:S(2)}, u32[]{:S(2)}) collective-permute-start(bf16[128,2048]{1,0:T(8,128)(2,1)} %bitcast.111), channel_id=1, source_target_pairs={{0,8},{8,16},{16,24},{24,32},{32,40},{40,48},{48,56},{56,64},{64,7... | collective-permute-start | bytes 1572872 | tf_op jit(solution)/shard_map/ppermute | solution.py:27
  302.6 111.8 %copy-start.1 = (bf16[1,128,2048]{2,1,0:T(8,128)(2,1)S(1)}, bf16[1,128,2048]{2,1,0:T(8,128)(2,1)}, u32[]{:S(2)}) copy-start(bf16[1,128,2048]{2,1,0:T(8,128)(2,1)} %param.18) | copy-start | bytes 1572868
  (4 other events, 4.8 us)
Sparse Core Ops, SparseCore 0:
  9.9 80.4 all-gather.1
  92.9 209.6 reduce-scatter.1
  305.2 107.2 all-reduce.7
where the time goes:
time: 427 us; the launch traced here: 421 us
  waiting for transfers between devices  304 us (71%)
  local copies, waits for them, and re-layouts  39.4 us (9%)
  matrix products  26.1 us (6%)
  starting transfers between devices  20.3 us (5%)
  between operations  15.5 us (4%)
  other arithmetic  15.3 us (4%)
    reduce_scatter x1, waiting for transfers between devices, per_device(): lax.psum_scatter(product * grad_factor, 'shard', scatter_dimension=0, til...  150 us
    psum x1, waiting for transfers between devices, per_device(): grad_w_out = lax.psum(shard_sum, 'rep')  105 us
    all_gather x1, waiting for transfers between devices, per_device(): shard_rows = lax.all_gather(w_out, 'shard', axis=0, tiled=True)  24.9 us
    ppermute x2, waiting for transfers between devices, extended_2(): lax.ppermute(lax.slice_in_dim(block, block.shape[dim] - width, None, axis...  17.1 us
    unnamed x43, local copies, waits for them, and re-layouts  11.2 us
    ppermute x4, starting transfers between devices, shifted(): lax.ppermute(value, axis, [(source, source + steps) for source in range(i...  10.3 us
    another operation x2, other arithmetic  8.66 us
  transfers between devices with their start and end apart: 11, of which 6 were waited for; matrix products, arithmetic and copies ran while one was open for 18% of the time, Pallas kernels for 0%

commit v1 on v0

v1 whole, which is shorter than its diff:
```python
import functools

import jax
import jax.numpy as jnp
from jax import lax
from jax.experimental import pallas as pl
from jax.experimental.pallas import tpu as pltpu
from jax.sharding import PartitionSpec as P

HEADS = 16
DH = 128
PATCH = 128
WIDTH = 2048
HALF = 1024
CHUNKS = 4
CW = WIDTH // CHUNKS
MESH = pl.DeviceIdType.MESH
F32 = jnp.float32
BF16 = jnp.bfloat16


def remote(src, dst, send, recv, target):
    return pltpu.make_async_remote_copy(
        src_ref=src, dst_ref=dst, send_sem=send, recv_sem=recv, device_id=target, device_id_type=MESH
    )


def kernel(
    factor,
    ids_ref,
    q_hbm,
    k_hbm,
    v_hbm,
    u_hbm,
    w_hbm,
    proj_ref,
    gq_ref,
    gk_ref,
    gv_ref,
    gw_ref,
    q_s,
    kw,
    vw,
    ubuf,
    tile,
    gsend,
    grecv,
    att,
    abuf,
    psend,
    precv,
    prob,
    prob_half,
    kts,
    vts,
    ktr,
    vtr,
    gw,
    ds,
    dr,
    xs,
    xr,
    zs,
    zr,
    fs,
    fr,
    local_sem,
    kv_send,
    kv_recv,
    y_send,
    y_recv,
    w_send,
    w_recv,
    t_send,
    t_recv,
    g_send,
    g_recv,
    f_send,
    f_recv,
):
    s = lax.axis_index("shard")
    r = lax.axis_index("rep")
    c = s % 2
    zl = (s // 2) % 4
    x = s // 8
    y = r % 4
    zh = r // 4
    z = zh * 4 + zl
    a = y // 2
    b = y % 2
    par = zl % 2
    zz = zl // 2

    def dev(dx, dy, zpos, core):
        return (dx * 8 + (zpos % 4) * 2 + core, (zpos // 4) * 4 + dy)

    ydev = [dev(x, (y + d) % 4, z, c) for d in range(4)]
    xdev = [dev((x + d) % 4, y, z, c) for d in range(4)]
    zdev = [dev(x, y, (z + d) % 8, c) for d in range(8)]
    sib = dev(x, y, z, 1 - c)
    left = (jnp.maximum(s - 1, 0), r)
    right = (jnp.minimum(s + 1, 31), r)
    has_left = s > 0
    has_right = s < 31

    loads = [
        pltpu.make_async_copy(q_hbm.at[0], q_s, local_sem.at[0]),
        pltpu.make_async_copy(k_hbm.at[0], kw.at[pl.ds(PATCH, PATCH)], local_sem.at[1]),
        pltpu.make_async_copy(v_hbm.at[0], vw.at[pl.ds(PATCH, PATCH)], local_sem.at[2]),
        pltpu.make_async_copy(
            u_hbm.at[0, :, pl.ds(pl.multiple_of(b * HALF, HALF), HALF)], ubuf.at[y], local_sem.at[3]
        ),
    ]
    for copy in loads:
        copy.start()
    wcols = pl.ds(pl.multiple_of(b * HALF, HALF), HALF)
    own_w = pltpu.make_async_copy(w_hbm.at[:, wcols], tile.at[2 * x + zz, c], local_sem.at[4])

    @pl.when(par == a)
    def _():
        own_w.start()

    barrier = pltpu.get_barrier_semaphore()

    def greet(target):
        pl.semaphore_signal(barrier, inc=1, device_id=target, device_id_type=MESH)

    for d in range(1, 4):
        greet(ydev[d])
        greet(xdev[d])
    for d in range(1, 8):
        greet(zdev[d])
    greet(sib)

    @pl.when(has_left)
    def _():
        greet(left)

    @pl.when(has_right)
    def _():
        greet(right)

    for bb in range(2):
        for zlow in range(2):
            for zhigh in range(2):
                sy = 2 * par + bb
                szl = 2 * zz + zlow
                same = (sy == y) & (szl == zl) & (zhigh == zh)

                @pl.when(jnp.logical_not(same))
                def _(sy=sy, szl=szl, zhigh=zhigh):
                    greet(dev(x, sy, zhigh * 4 + szl, c))

    wait_for = (
        14
        + jnp.where(has_left, 1, 0)
        + jnp.where(has_right, 1, 0)
        + jnp.where(par == a, 7, 8)
    )
    pl.semaphore_wait(barrier, wait_for)

    zoff = [1, 7, jnp.where(c == 0, 2, 6)]

    @pl.when(par == a)
    def _():
        for i, d in enumerate(zoff):
            remote(
                w_hbm.at[:, wcols],
                tile.at[2 * x + zz, c],
                w_send.at[i],
                w_recv.at[i],
                dev(x, y, (z + d) % 8, c),
            ).start()

    def halo(i, k, direction):
        src, dst = ((k_hbm, kw), (v_hbm, vw))[k]
        cols = pl.ds(i * CW, CW)
        rows = pl.ds(0 if direction else 2 * PATCH, PATCH)
        index = (i * 2 + k) * 2 + direction
        return remote(
            src.at[0, :, cols],
            dst.at[rows, cols],
            kv_send.at[index],
            kv_recv.at[index],
            right if direction else left,
        )

    for i in range(CHUNKS):
        for k in range(2):

            @pl.when(has_left)
            def _(i=i, k=k):
                halo(i, k, 0).start()

            @pl.when(has_right)
            def _(i=i, k=k):
                halo(i, k, 1).start()

    def ycopy(kind, d, src, dst_buf, slot):
        return remote(src, dst_buf.at[slot], y_send.at[kind, d - 1], y_recv.at[kind, d - 1], ydev[d])

    def u_piece(d):
        bb = ((y + d) % 4) % 2
        return u_hbm.at[0, :, pl.ds(pl.multiple_of(bb * HALF, HALF), HALF)]

    for d in (1, 3, 2):
        ycopy(0, d, u_piece(d), ubuf, y).start()

    def ywait_recv(kind, d, src, dst_buf):
        ycopy(kind, d, src, dst_buf, (y - d + 4) % 4).wait_recv()

    @pl.when(jnp.logical_not(has_left))
    def _():
        kw[0:PATCH, :] = jnp.zeros((PATCH, WIDTH), BF16)
        vw[0:PATCH, :] = jnp.zeros((PATCH, WIDTH), BF16)
        ktr[0] = jnp.zeros((PATCH, WIDTH), BF16)
        vtr[0] = jnp.zeros((PATCH, WIDTH), BF16)

    @pl.when(jnp.logical_not(has_right))
    def _():
        kw[2 * PATCH :, :] = jnp.zeros((PATCH, WIDTH), BF16)
        vw[2 * PATCH :, :] = jnp.zeros((PATCH, WIDTH), BF16)
        ktr[1] = jnp.zeros((PATCH, WIDTH), BF16)
        vtr[1] = jnp.zeros((PATCH, WIDTH), BF16)

    def wz_wait(i):
        d = zoff[i]
        szl = (z - d + 8) % 4
        remote(
            w_hbm.at[:, wcols],
            tile.at[2 * x + szl // 2, c],
            w_send.at[i],
            w_recv.at[i],
            sib,
        ).wait_recv()

    @pl.when(par == a)
    def _():
        own_w.wait()
        wz_wait(2)

    @pl.when(par != a)
    def _():
        wz_wait(0)
        wz_wait(1)

    def wx(d):
        part = tile.at[pl.ds(2 * x, 2), c]
        return remote(part, part, w_send.at[2 + d], w_recv.at[2 + d], xdev[d])

    def wx_wait(d):
        part = tile.at[pl.ds(2 * ((x - d + 4) % 4), 2), c]
        remote(part, part, w_send.at[2 + d], w_recv.at[2 + d], xdev[d]).wait_recv()

    for d in (1, 3, 2):
        wx(d).start()
    for d in (1, 3, 2):
        wx_wait(d)
    to_sib = remote(tile.at[:, c], tile.at[:, c], w_send.at[6], w_recv.at[6], sib)
    to_sib.start()
    from_sib = remote(tile.at[:, 1 - c], tile.at[:, 1 - c], w_send.at[6], w_recv.at[6], sib)
    from_sib.wait_recv()

    loads[3].wait()
    for d in (1, 3, 2):
        ywait_recv(0, d, u_piece(d), ubuf)
    nodes_u = ubuf[...].reshape(4 * PATCH, HALF)
    for j in range(4):
        rows = tile[2 * j : 2 * j + 2].reshape(256, HALF)
        part = lax.dot_general(nodes_u, rows, (((1,), (1,)), ((), ())), preferred_element_type=F32)
        gsend[:, :, 256 * j : 256 * j + 256] = part.astype(BF16).reshape(4, PATCH, 256)
    for d in (1, 3, 2):
        ycopy(1, d, gsend.at[(y + d) % 4], grecv, y).start()
    grecv[y] = gsend[y]

    for copy in loads[:3]:
        copy.wait()
    left_ok = ids_ref[0, 0, 0] != s
    right_ok = ids_ref[0, 0, 1] != s
    at = lax.broadcasted_iota(jnp.int32, (PATCH, 3 * PATCH), 1)
    allowed = ((at >= PATCH) | left_ok) & ((at < 2 * PATCH) | right_ok)
    scaling = DH ** (-0.5)

    def forward_head(h, half, t):
        cols = pl.ds(pl.multiple_of(h * DH, DH), DH)
        scores = (
            lax.dot_general(q_s[:, cols], kw[:, cols], (((1,), (1,)), ((), ())), preferred_element_type=F32)
            * scaling
        )
        highest = jnp.max(jnp.where(allowed, scores, -jnp.inf), axis=-1, keepdims=True)
        numer = jnp.where(allowed, jnp.exp(scores - highest), 0.0)
        total = jnp.sum(numer, axis=-1, keepdims=True)
        p = numer / total
        ph = p.astype(BF16)
        prob[h] = p
        prob_half[h] = ph
        out = jnp.dot(ph, vw[:, cols], preferred_element_type=F32)
        att[half, :, pl.ds(pl.multiple_of(t * DH, DH), DH)] = out.astype(BF16)

    per = HEADS // 2 // CHUNKS

    for i in range(CHUNKS):
        for k in range(2):

            @pl.when(has_left)
            def _(i=i, k=k):
                halo(i, k, 1).wait_recv()

            @pl.when(has_right)
            def _(i=i, k=k):
                halo(i, k, 0).wait_recv()

        @pl.loop(i * per, (i + 1) * per)
        def _(t):
            for half in range(2):
                forward_head(2 * t + half, half, t)

    def a_piece(d):
        return att.at[((y + d) % 4) // 2]

    for d in (1, 3, 2):
        ycopy(2, d, a_piece(d), abuf, y).start()
    abuf[y] = att[a]

    for d in (1, 3, 2):
        ywait_recv(1, d, gsend.at[(y + d) % 4], grecv)

    def term(i, k, direction):
        src, dst = ((kts, ktr), (vts, vtr))[k]
        cols = pl.ds(i * CW, CW)
        index = (i * 2 + k) * 2 + direction
        return remote(
            src.at[2 * direction, :, cols],
            dst.at[1 - direction, :, cols],
            t_send.at[index],
            t_recv.at[index],
            right if direction else left,
        )

    def backward_head(h, half, t):
        cols = pl.ds(pl.multiple_of(h * DH, DH), DH)
        tc = pl.ds(pl.multiple_of(t * DH, DH), DH)
        ga = (grecv[2 * half, :, tc].astype(F32) + grecv[2 * half + 1, :, tc].astype(F32)).astype(BF16)
        p = prob[h]
        pg = lax.dot_general(ga, vw[:, cols], (((1,), (1,)), ((), ())), preferred_element_type=F32)
        delta = jnp.sum(p * pg, axis=-1, keepdims=True)
        sg = (p * (pg - delta)).astype(BF16)
        gq_ref[0, :, cols] = (jnp.dot(sg, kw[:, cols], preferred_element_type=F32) * scaling).astype(BF16)
        kt = (
            lax.dot_general(sg, q_s[:, cols], (((0,), (0,)), ((), ())), preferred_element_type=F32) * scaling
        ).astype(BF16)
        vt = lax.dot_general(
            prob_half[h], ga, (((0,), (0,)), ((), ())), preferred_element_type=F32
        ).astype(BF16)
        kts[:, :, cols] = kt.reshape(3, PATCH, DH)
        vts[:, :, cols] = vt.reshape(3, PATCH, DH)

    for i in range(CHUNKS):

        @pl.loop(i * per, (i + 1) * per)
        def _(t):
            for half in range(2):
                backward_head(2 * t + half, half, t)

        for k in range(2):

            @pl.when(has_left)
            def _(i=i, k=k):
                term(i, k, 0).start()

            @pl.when(has_right)
            def _(i=i, k=k):
                term(i, k, 1).start()

    for d in (1, 3, 2):
        ywait_recv(2, d, a_piece(d), abuf)
    nodes_u = ubuf[...].reshape(4 * PATCH, HALF)
    for j in range(4):
        cols_a = abuf[:, :, 256 * j : 256 * j + 256].reshape(4 * PATCH, 256)
        part = lax.dot_general(cols_a, nodes_u, (((0,), (0,)), ((), ())), preferred_element_type=F32)
        gw[2 * j : 2 * j + 2] = part.reshape(2, 2, 64, HALF)
    ds[...] = gw[:, 1 - c].astype(BF16)
    d_copy = remote(ds, dr, g_send.at[0], g_recv.at[0], sib)
    d_copy.start()

    nodes_a = abuf[...].reshape(4 * PATCH, HALF)
    weights = tile[...].reshape(HALF, HALF)
    for j in range(4):
        part = jnp.dot(nodes_a, weights[:, 256 * j : 256 * j + 256], preferred_element_type=F32)
        psend[:, :, 256 * j : 256 * j + 256] = part.astype(BF16).reshape(4, PATCH, 256)
    for d in (1, 3, 2):
        ycopy(3, d, psend.at[(y + d) % 4], precv, y).start()
    precv[y] = psend[y]

    d_copy.wait_recv()
    xs[...] = (gw[:, c] + dr[...].astype(F32)).astype(BF16)

    def x_copy(d):
        return remote(
            xs.at[pl.ds(2 * ((x + d) % 4), 2)], xr.at[d - 1], g_send.at[d], g_recv.at[d], xdev[d]
        )

    for d in (1, 3, 2):
        x_copy(d).start()
    for d in (1, 3, 2):
        x_copy(d).wait_recv()
    own = gw[pl.ds(2 * x, 2), c] + dr[pl.ds(2 * x, 2)].astype(F32)
    for d in range(3):
        own += xr[d].astype(F32)
    zs[...] = own.astype(BF16)

    def z_piece(d):
        to = (z + d) % 8
        quarter = (to // 4) * 2 + to % 2
        return zs.at[(to % 4) // 2, pl.ds(pl.multiple_of(quarter * 16, 16), 16)]

    def z_copy(d):
        return remote(z_piece(d), zr.at[d - 1], g_send.at[3 + d], g_recv.at[3 + d], zdev[d])

    for d in (4, 3, 5, 2, 6, 1, 7):
        z_copy(d).start()
    quarter = zh * 2 + par
    mine = zs[zz, pl.ds(pl.multiple_of(quarter * 16, 16), 16)].astype(F32)
    for d in range(1, 8):
        z_copy(d).wait_recv()
    for d in range(7):
        mine += zr[d].astype(F32)
    fs[...] = (mine * factor).astype(BF16)

    szl = 2 * zz + a

    def spread(zhigh, dy, slot):
        return remote(
            fs,
            fr.at[quarter, b],
            f_send.at[slot],
            f_recv.at[2 * quarter + b],
            dev(x, dy, zhigh * 4 + szl, c),
        )

    def spread_same(zhigh, dy):
        return (par == a) & (zhigh == zh) & (dy == y)

    for zhigh in range(2):
        for dy in range(4):

            @pl.when(jnp.logical_not(spread_same(zhigh, dy)))
            def _(zhigh=zhigh, dy=dy):
                spread(zhigh, dy, zhigh * 4 + dy).start()

    @pl.when(par == a)
    def _():
        fr[quarter, b] = fs[...]

    for d in (1, 3, 2):
        ywait_recv(3, d, psend.at[(y + d) % 4], precv)
    for bb in range(2):
        proj_ref[0, :, bb * HALF : (bb + 1) * HALF] = (
            precv[bb].astype(F32) + precv[2 + bb].astype(F32)
        ).astype(BF16)

    for i in range(CHUNKS):
        for k in range(2):

            @pl.when(has_left)
            def _(i=i, k=k):
                term(i, k, 1).wait_recv()

            @pl.when(has_right)
            def _(i=i, k=k):
                term(i, k, 0).wait_recv()

    gk_ref[0] = (kts[1].astype(F32) + ktr[0].astype(F32) + ktr[1].astype(F32)).astype(BF16)
    gv_ref[0] = (vts[1].astype(F32) + vtr[0].astype(F32) + vtr[1].astype(F32)).astype(BF16)

    for qq in range(4):
        for bb in range(2):
            same = (par == a) & (qq == quarter) & (bb == b)

            @pl.when(jnp.logical_not(same))
            def _(qq=qq, bb=bb):
                remote(
                    fs, fr.at[qq, bb], f_send.at[0], f_recv.at[2 * qq + bb], sib
                ).wait_recv()

    for qq in range(4):
        for bb in range(2):
            gw_ref[16 * qq : 16 * qq + 16, bb * HALF : (bb + 1) * HALF] = fr[qq, bb].astype(F32)

    @pl.when(par == a)
    def _():
        for i in range(3):
            remote(w_hbm.at[:, wcols], tile.at[2 * x + zz, c], w_send.at[i], w_recv.at[i], sib).wait_send()

    for d in range(1, 4):
        wx(d).wait_send()
        ycopy(0, d, u_piece(d), ubuf, y).wait_send()
        ycopy(1, d, gsend.at[(y + d) % 4], grecv, y).wait_send()
        ycopy(2, d, a_piece(d), abuf, y).wait_send()
        ycopy(3, d, psend.at[(y + d) % 4], precv, y).wait_send()
        x_copy(d).wait_send()
    to_sib.wait_send()
    d_copy.wait_send()
    for d in range(1, 8):
        z_copy(d).wait_send()
    for i in range(CHUNKS):
        for k in range(2):

            @pl.when(has_left)
            def _(i=i, k=k):
                halo(i, k, 0).wait_send()
                term(i, k, 0).wait_send()

            @pl.when(has_right)
            def _(i=i, k=k):
                halo(i, k, 1).wait_send()
                term(i, k, 1).wait_send()

    for zhigh in range(2):
        for dy in range(4):

            @pl.when(jnp.logical_not(spread_same(zhigh, dy)))
            def _(zhigh=zhigh, dy=dy):
                spread(zhigh, dy, zhigh * 4 + dy).wait_send()


def per_device(queries, key_vectors, value_vectors, neighbor_ids, upstream, w_out):
    factor = float(8 * 4096) ** (-0.5)
    rows = jax.ShapeDtypeStruct((1, PATCH, WIDTH), BF16)
    dma = pltpu.SemaphoreType.DMA
    vmem = pltpu.VMEM
    out = pl.pallas_call(
        functools.partial(kernel, factor),
        out_shape=(rows, rows, rows, rows, jax.ShapeDtypeStruct((64, WIDTH), F32)),
        in_specs=[pl.BlockSpec(memory_space=pltpu.SMEM)] + [pl.BlockSpec(memory_space=pl.ANY)] * 5,
        out_specs=[pl.BlockSpec(memory_space=pltpu.VMEM)] * 5,
        scratch_shapes=[
            vmem((PATCH, WIDTH), BF16),
            vmem((3 * PATCH, WIDTH), BF16),
            vmem((3 * PATCH, WIDTH), BF16),
            vmem((4, PATCH, HALF), BF16),
            vmem((8, 2, 64, HALF), BF16),
            vmem((4, PATCH, HALF), BF16),
            vmem((4, PATCH, HALF), BF16),
            vmem((2, PATCH, HALF), BF16),
            vmem((4, PATCH, HALF), BF16),
            vmem((4, PATCH, HALF), BF16),
            vmem((4, PATCH, HALF), BF16),
            vmem((HEADS, PATCH, 3 * PATCH), F32),
            vmem((HEADS, PATCH, 3 * PATCH), BF16),
            vmem((3, PATCH, WIDTH), BF16),
            vmem((3, PATCH, WIDTH), BF16),
            vmem((2, PATCH, WIDTH), BF16),
            vmem((2, PATCH, WIDTH), BF16),
            vmem((8, 2, 64, HALF), F32),
            vmem((8, 64, HALF), BF16),
            vmem((8, 64, HALF), BF16),
            vmem((8, 64, HALF), BF16),
            vmem((3, 2, 64, HALF), BF16),
            vmem((2, 64, HALF), BF16),
            vmem((7, 16, HALF), BF16),
            vmem((16, HALF), BF16),
            vmem((4, 2, 16, HALF), BF16),
            dma((5,)),
            dma((4 * CHUNKS,)),
            dma((4 * CHUNKS,)),
            dma((4, 3)),
            dma((4, 3)),
            dma((7,)),
            dma((7,)),
            dma((4 * CHUNKS,)),
            dma((4 * CHUNKS,)),
            dma((11,)),
            dma((11,)),
            dma((8,)),
            dma((8,)),
        ],
        compiler_params=pltpu.CompilerParams(
            collective_id=0, has_side_effects=True, vmem_limit_bytes=56 * 1024 * 1024
        ),
        cost_estimate=pl.CostEstimate(flops=5_000_000_000, bytes_accessed=6_000_000, transcendentals=800_000),
        name="mesh_attention",
    )(neighbor_ids, queries, key_vectors, value_vectors, upstream, w_out)
    return tuple(out)


def solution(mesh):
    rows = P("rep", "shard", None)
    return jax.shard_map(
        per_device,
        mesh=mesh,
        in_specs=(rows, rows, rows, rows, rows, P("shard", None)),
        out_specs=(rows, rows, rows, rows, P("shard", None)),
        check_vma=False,
    )
```

time: 427 us -> 115 us (0.27); the launches traced: 421 us -> 113 us
  waiting for transfers between devices: 304 us -> 0 us
  Pallas kernels: 0 us -> 106 us
  local copies, waits for them, and re-layouts: 39.4 us -> 6.42 us
  matrix products: 26.1 us -> 0 us
  starting transfers between devices: 20.3 us -> 0 us
  other arithmetic: 15.3 us -> 0 us
  between operations: 15.5 us -> 0.66 us
    reduce_scatter x1 -> x0, waiting for transfers between devices: 150 us -> none  [per_device(): lax.psum_scatter(product * grad_factor, 'shard', scatter_dimension=0, til...]
    pallas_call x0 -> x1, Pallas kernels: none -> 106 us  [per_device(): pl.pallas_call(functools.partial(kernel, factor), out_shape=(rows, rows,...]
    psum x1 -> x0, waiting for transfers between devices: 105 us -> none  [per_device(): grad_w_out = lax.psum(shard_sum, 'rep')]
    dot_general x9 -> x0, matrix products: 26.1 us -> none  [the longest x1 8.14 us: per_device(): lax.dot_general(columns, upstream_rows, (((0,), (0,)), ((), ())), preferr...]
    all_gather x1 -> x0, waiting for transfers between devices: 24.9 us -> none  [per_device(): shard_rows = lax.all_gather(w_out, 'shard', axis=0, tiled=True)]
    ppermute x8 -> x0, waiting for transfers between devices: 23.4 us -> none  [the longest x2 17.1 us: extended_2(): lax.ppermute(lax.slice_in_dim(block, block.shape[dim] - width, None, axis...]
    ppermute x8 -> x0, starting transfers between devices: 20 us -> none  [the longest x4 10.3 us: shifted(): lax.ppermute(value, axis, [(source, source + steps) for source in range(i...]
    slice x8 -> x0, local copies, waits for them, and re-layouts: 13.8 us -> none  [the longest x1 3.34 us: per_device(): inner_values = value_sums[1:local_count + 1]]
  transfers between devices with their start and end apart: 11 -> 0, of which waited for: 6 -> 0; matrix products, arithmetic and copies ran while one was open for 18% -> 0% of each run, Pallas kernels for 0% -> 0%
where the time goes in v1:
time: 115 us; the launch traced here: 113 us
  Pallas kernels  106 us (92%)
  local copies, waits for them, and re-layouts  6.42 us (6%)
    pallas_call x1, Pallas kernels, per_device(): pl.pallas_call(functools.partial(kernel, factor), out_shape=(rows, rows,...  106 us
    unnamed x13, local copies, waits for them, and re-layouts  6.42 us

profile of v1, /device:TPU:90, one launch (start us, length us, event | category | flops | bytes accessed | tf_op | source)
XLA Modules:
  0.0 113.3 jit_solution(721551959684382795)
XLA Ops:
  0.6 106.2 %mesh_attention.1 = (bf16[1,128,2048]{2,1,0:T(8,128)(2,1)}, bf16[1,128,2048]{2,1,0:T(8,128)(2,1)}, bf16[1,128,2048]{2,1,0:T(8,128)(2,1)}, bf16[1,128,2048]{2,1,0:T(8,128)(2,1)}, f32[64,2048]{1,0:T(8,128)}) custom-call(s32[1,1,2]{2,1,0:T(1,128)} %ids_ref.1, bf16[1,128,2048]{2,1,0:T(8,128)(2,1)} %q_hbm.1, bf16[1,128,2048]{2,1,0:T(8,128)(2,1)} %k_hbm.1, ...), custom_call_target="tpu_custom_call" | custom-call | flops 5000000000 | bytes 6000000 | tf_op jit(solution)/shard_map/mesh_attention/pallas_call | solution.py:532
  106.8 0.0 copy-start.3
  106.8 1.9 %copy.16 = bf16[1,128,2048]{2,1,0:T(8,128)(2,1)} copy(bf16[1,128,2048]{2,1,0:T(8,128)(2,1)} %get-tuple-element.10) | data formatting | bytes 1048576
  108.8 0.0 copy-done.3
  108.8 0.0 copy-start.2
  108.8 0.8 copy.17
  109.6 0.4 copy-done.2
  110.0 0.0 copy-start.1
  110.0 0.8 copy.18
  110.8 0.4 copy-done.1
  111.2 0.0 copy-start
  111.2 0.8 copy.19
  112.0 0.4 copy-done
  112.5 0.8 copy.20
Async XLA Ops:
  106.8 2.0 %copy-start.3 = (bf16[1,128,2048]{2,1,0:T(8,128)(2,1)S(1)}, bf16[1,128,2048]{2,1,0:T(8,128)(2,1)}, u32[]{:S(2)}) copy-start(bf16[1,128,2048]{2,1,0:T(8,128)(2,1)} %get-tuple-element.11) | copy-start | bytes 1572868
  108.8 1.2 %copy-start.2 = (bf16[1,128,2048]{2,1,0:T(8,128)(2,1)S(1)}, bf16[1,128,2048]{2,1,0:T(8,128)(2,1)}, u32[]{:S(2)}) copy-start(bf16[1,128,2048]{2,1,0:T(8,128)(2,1)} %get-tuple-element.12) | copy-start | bytes 1572868
  110.0 1.2 %copy-start.1 = (bf16[1,128,2048]{2,1,0:T(8,128)(2,1)S(1)}, bf16[1,128,2048]{2,1,0:T(8,128)(2,1)}, u32[]{:S(2)}) copy-start(bf16[1,128,2048]{2,1,0:T(8,128)(2,1)} %get-tuple-element.13) | copy-start | bytes 1572868
  111.2 1.2 %copy-start = (f32[64,2048]{1,0:T(8,128)S(1)}, f32[64,2048]{1,0:T(8,128)}, u32[]{:S(2)}) copy-start(f32[64,2048]{1,0:T(8,128)} %get-tuple-element.14) | copy-start | bytes 1572868

commit v2 on v1

--- a/solution.py
+++ b/solution.py
@@ -14,6 +14,8 @@
 HALF = 1024
 CHUNKS = 4
 CW = WIDTH // CHUNKS
+TW = HALF // CHUNKS
+ORDER = (0, 1, 3, 2)
 MESH = pl.DeviceIdType.MESH
 F32 = jnp.float32
 BF16 = jnp.bfloat16
@@ -69,6 +71,12 @@
     kv_recv,
     y_send,
     y_recv,
+    a_send,
+    a_recv,
+    gy_send,
+    gy_recv,
+    wd_send,
+    wd_recv,
     w_send,
     w_recv,
     t_send,
@@ -100,6 +108,8 @@
     sib = dev(x, y, z, 1 - c)
     left = (jnp.maximum(s - 1, 0), r)
     right = (jnp.minimum(s + 1, 31), r)
+    x_left = jnp.maximum(s - 1, 0) // 8
+    x_right = jnp.minimum(s + 1, 31) // 8
     has_left = s > 0
     has_right = s < 31
 
@@ -172,9 +182,12 @@
                 dev(x, y, (z + d) % 8, c),
             ).start()
 
-    def halo(i, k, direction):
+    def chunk(at_x, i):
+        return (at_x + ORDER[i]) % 4
+
+    def halo(i, k, direction, at_x):
         src, dst = ((k_hbm, kw), (v_hbm, vw))[k]
-        cols = pl.ds(i * CW, CW)
+        cols = pl.ds(pl.multiple_of(chunk(at_x, i) * CW, CW), CW)
         rows = pl.ds(0 if direction else 2 * PATCH, PATCH)
         index = (i * 2 + k) * 2 + direction
         return remote(
@@ -185,16 +198,30 @@
             right if direction else left,
         )
 
+    def halo_start(i):
+        for k in range(2):
+
+            @pl.when(has_left)
+            def _(k=k):
+                halo(i, k, 0, x_left).start()
+
+            @pl.when(has_right)
+            def _(k=k):
+                halo(i, k, 1, x_right).start()
+
+    def halo_wait(i):
+        for k in range(2):
+
+            @pl.when(has_left)
+            def _(k=k):
+                halo(i, k, 1, x).wait_recv()
+
+            @pl.when(has_right)
+            def _(k=k):
+                halo(i, k, 0, x).wait_recv()
+
     for i in range(CHUNKS):
-        for k in range(2):
-
-            @pl.when(has_left)
-            def _(i=i, k=k):
-                halo(i, k, 0).start()
-
-            @pl.when(has_right)
-            def _(i=i, k=k):
-                halo(i, k, 1).start()
+        halo_start(i)
 
     def ycopy(kind, d, src, dst_buf, slot):
         return remote(src, dst_buf.at[slot], y_send.at[kind, d - 1], y_recv.at[kind, d - 1], ydev[d])
@@ -254,24 +281,6 @@
 
     for d in (1, 3, 2):
         wx(d).start()
-    for d in (1, 3, 2):
-        wx_wait(d)
-    to_sib = remote(tile.at[:, c], tile.at[:, c], w_send.at[6], w_recv.at[6], sib)
-    to_sib.start()
-    from_sib = remote(tile.at[:, 1 - c], tile.at[:, 1 - c], w_send.at[6], w_recv.at[6], sib)
-    from_sib.wait_recv()
-
-    loads[3].wait()
-    for d in (1, 3, 2):
-        ywait_recv(0, d, u_piece(d), ubuf)
-    nodes_u = ubuf[...].reshape(4 * PATCH, HALF)
-    for j in range(4):
-        rows = tile[2 * j : 2 * j + 2].reshape(256, HALF)
-        part = lax.dot_general(nodes_u, rows, (((1,), (1,)), ((), ())), preferred_element_type=F32)
-        gsend[:, :, 256 * j : 256 * j + 256] = part.astype(BF16).reshape(4, PATCH, 256)
-    for d in (1, 3, 2):
-        ycopy(1, d, gsend.at[(y + d) % 4], grecv, y).start()
-    grecv[y] = gsend[y]
 
     for copy in loads[:3]:
         copy.wait()
@@ -280,6 +289,7 @@
     at = lax.broadcasted_iota(jnp.int32, (PATCH, 3 * PATCH), 1)
     allowed = ((at >= PATCH) | left_ok) & ((at < 2 * PATCH) | right_ok)
     scaling = DH ** (-0.5)
+    per = HEADS // 2 // CHUNKS
 
     def forward_head(h, half, t):
         cols = pl.ds(pl.multiple_of(h * DH, DH), DH)
@@ -297,37 +307,84 @@
         out = jnp.dot(ph, vw[:, cols], preferred_element_type=F32)
         att[half, :, pl.ds(pl.multiple_of(t * DH, DH), DH)] = out.astype(BF16)
 
-    per = HEADS // 2 // CHUNKS
-
-    for i in range(CHUNKS):
-        for k in range(2):
-
-            @pl.when(has_left)
-            def _(i=i, k=k):
-                halo(i, k, 1).wait_recv()
-
-            @pl.when(has_right)
-            def _(i=i, k=k):
-                halo(i, k, 0).wait_recv()
-
-        @pl.loop(i * per, (i + 1) * per)
-        def _(t):
+    def tcols(i):
+        return pl.ds(pl.multiple_of(chunk(x, i) * TW, TW), TW)
+
+    def a_copy(i, d, slot):
+        return remote(
+            att.at[((y + d) % 4) // 2, :, tcols(i)],
+            abuf.at[slot, :, tcols(i)],
+            a_send.at[i, d - 1],
+            a_recv.at[i, d - 1],
+            ydev[d],
+        )
+
+    def forward(i):
+        halo_wait(i)
+        first = chunk(x, i) * per
+
+        @pl.loop(0, per)
+        def _(n):
             for half in range(2):
-                forward_head(2 * t + half, half, t)
-
-    def a_piece(d):
-        return att.at[((y + d) % 4) // 2]
-
-    for d in (1, 3, 2):
-        ycopy(2, d, a_piece(d), abuf, y).start()
-    abuf[y] = att[a]
-
-    for d in (1, 3, 2):
-        ywait_recv(1, d, gsend.at[(y + d) % 4], grecv)
-
-    def term(i, k, direction):
+                forward_head(2 * (first + n) + half, half, first + n)
+
+        for d in (1, 3, 2):
+            a_copy(i, d, y).start()
+        abuf[y, :, tcols(i)] = att[a, :, tcols(i)]
+
+    def wd_copy(i, core):
+        part = tile.at[pl.ds(2 * chunk(x, i), 2), core]
+        return remote(part, part, wd_send.at[i], wd_recv.at[i], sib)
+
+    def tile_ready(i):
+        if i > 0:
+            wx_wait((4 - ORDER[i]) % 4)
+        wd_copy(i, c).start()
+
+    def g_copy(i, d, slot):
+        return remote(
+            gsend.at[(y + d) % 4, :, tcols(i)],
+            grecv.at[slot, :, tcols(i)],
+            gy_send.at[i, d - 1],
+            gy_recv.at[i, d - 1],
+            ydev[d],
+        )
+
+    def upstream_part(i):
+        wd_copy(i, 1 - c).wait_recv()
+        rows = tile[pl.ds(2 * chunk(x, i), 2)].reshape(TW, HALF)
+        nodes = ubuf[...].reshape(4 * PATCH, HALF)
+        part = lax.dot_general(nodes, rows, (((1,), (1,)), ((), ())), preferred_element_type=F32)
+        gsend[:, :, tcols(i)] = part.astype(BF16).reshape(4, PATCH, TW)
+        for d in (1, 3, 2):
+            g_copy(i, d, y).start()
+        grecv[y, :, tcols(i)] = gsend[y, :, tcols(i)]
+
+    def d_copy(i):
+        return remote(ds.at[i], dr.at[i], g_send.at[i], g_recv.at[i], sib)
+
+    def x_copy(i):
+        d = ORDER[i]
+        return remote(xs.at[i - 1], xr.at[d - 1], g_send.at[3 + d], g_recv.at[3 + d], xdev[d])
+
+    def gradient(i):
+        for d in (1, 3, 2):
+            a_copy(i, d, (y - d + 4) % 4).wait_recv()
+        cols_a = abuf[:, :, tcols(i)].reshape(4 * PATCH, TW)
+        nodes_u = ubuf[...].reshape(4 * PATCH, HALF)
+        part = lax.dot_general(cols_a, nodes_u, (((0,), (0,)), ((), ())), preferred_element_type=F32)
+        gw[i] = part.reshape(2, 2, 64, HALF)
+        ds[i] = gw[i, :, 1 - c].astype(BF16)
+        d_copy(i).start()
+
+    def over_x(i):
+        d_copy(i).wait_recv()
+        xs[i - 1] = (gw[i, :, c] + dr[i].astype(F32)).astype(BF16)
+        x_copy(i).start()
+
+    def term(i, k, direction, at_x):
         src, dst = ((kts, ktr), (vts, vtr))[k]
-        cols = pl.ds(i * CW, CW)
+        cols = pl.ds(pl.multiple_of(chunk(at_x, i) * CW, CW), CW)
         index = (i * 2 + k) * 2 + direction
         return remote(
             src.at[2 * direction, :, cols],
@@ -355,33 +412,51 @@
         kts[:, :, cols] = kt.reshape(3, PATCH, DH)
         vts[:, :, cols] = vt.reshape(3, PATCH, DH)
 
-    for i in range(CHUNKS):
-
-        @pl.loop(i * per, (i + 1) * per)
-        def _(t):
+    def backward(i):
+        first = chunk(x, i) * per
+        for d in (1, 3, 2):
+            g_copy(i, d, (y - d + 4) % 4).wait_recv()
+
+        @pl.loop(0, per)
+        def _(n):
             for half in range(2):
-                backward_head(2 * t + half, half, t)
+                backward_head(2 * (first + n) + half, half, first + n)
 
         for k in range(2):
 
             @pl.when(has_left)
-            def _(i=i, k=k):
-                term(i, k, 0).start()
+            def _(k=k):
+                term(i, k, 0, x).start()
 
             @pl.when(has_right)
-            def _(i=i, k=k):
-                term(i, k, 1).start()
-
+            def _(k=k):
+                term(i, k, 1, x).start()
+
+    tile_ready(0)
+    forward(0)
+    loads[3].wait()
     for d in (1, 3, 2):
-        ywait_recv(2, d, a_piece(d), abuf)
-    nodes_u = ubuf[...].reshape(4 * PATCH, HALF)
-    for j in range(4):
-        cols_a = abuf[:, :, 256 * j : 256 * j + 256].reshape(4 * PATCH, 256)
-        part = lax.dot_general(cols_a, nodes_u, (((0,), (0,)), ((), ())), preferred_element_type=F32)
-        gw[2 * j : 2 * j + 2] = part.reshape(2, 2, 64, HALF)
-    ds[...] = gw[:, 1 - c].astype(BF16)
-    d_copy = remote(ds, dr, g_send.at[0], g_recv.at[0], sib)
-    d_copy.start()
+        ywait_recv(0, d, u_piece(d), ubuf)
+    upstream_part(0)
+    tile_ready(1)
+    forward(1)
+    upstream_part(1)
+    backward(0)
+    tile_ready(2)
+    forward(2)
+    upstream_part(2)
+    gradient(0)
+    backward(1)
+    tile_ready(3)
+    forward(3)
+    upstream_part(3)
+    gradient(1)
+    gradient(2)
+    over_x(1)
+    backward(2)
+    gradient(3)
+    over_x(2)
+    over_x(3)
 
     nodes_a = abuf[...].reshape(4 * PATCH, HALF)
     weights = tile[...].reshape(HALF, HALF)
@@ -389,22 +464,15 @@
         part = jnp.dot(nodes_a, weights[:, 256 * j : 256 * j + 256], preferred_element_type=F32)
         psend[:, :, 256 * j : 256 * j + 256] = part.astype(BF16).reshape(4, PATCH, 256)
     for d in (1, 3, 2):
-        ycopy(3, d, psend.at[(y + d) % 4], precv, y).start()
+        ycopy(1, d, psend.at[(y + d) % 4], precv, y).start()
     precv[y] = psend[y]
 
-    d_copy.wait_recv()
-    xs[...] = (gw[:, c] + dr[...].astype(F32)).astype(BF16)
-
-    def x_copy(d):
-        return remote(
-            xs.at[pl.ds(2 * ((x + d) % 4), 2)], xr.at[d - 1], g_send.at[d], g_recv.at[d], xdev[d]
-        )
-
-    for d in (1, 3, 2):
-        x_copy(d).start()
-    for d in (1, 3, 2):
-        x_copy(d).wait_recv()
-    own = gw[pl.ds(2 * x, 2), c] + dr[pl.ds(2 * x, 2)].astype(F32)
+    backward(3)
+
+    d_copy(0).wait_recv()
+    own = gw[0, :, c] + dr[0].astype(F32)
+    for i in range(1, CHUNKS):
+        x_copy(i).wait_recv()
     for d in range(3):
         own += xr[d].astype(F32)
     zs[...] = own.astype(BF16)
@@ -415,10 +483,11 @@
         return zs.at[(to % 4) // 2, pl.ds(pl.multiple_of(quarter * 16, 16), 16)]
 
     def z_copy(d):
-        return remote(z_piece(d), zr.at[d - 1], g_send.at[3 + d], g_recv.at[3 + d], zdev[d])
+        return remote(z_piece(d), zr.at[d - 1], g_send.at[6 + d], g_recv.at[6 + d], zdev[d])
 
     for d in (4, 3, 5, 2, 6, 1, 7):
         z_copy(d).start()
+
     quarter = zh * 2 + par
     mine = zs[zz, pl.ds(pl.multiple_of(quarter * 16, 16), 16)].astype(F32)
     for d in range(1, 8):
@@ -453,7 +522,7 @@
         fr[quarter, b] = fs[...]
 
     for d in (1, 3, 2):
-        ywait_recv(3, d, psend.at[(y + d) % 4], precv)
+        ywait_recv(1, d, psend.at[(y + d) % 4], precv)
     for bb in range(2):
         proj_ref[0, :, bb * HALF : (bb + 1) * HALF] = (
             precv[bb].astype(F32) + precv[2 + bb].astype(F32)
@@ -464,11 +533,11 @@
 
             @pl.when(has_left)
             def _(i=i, k=k):
-                term(i, k, 1).wait_recv()
+                term(i, k, 1, x_left).wait_recv()
 
             @pl.when(has_right)
             def _(i=i, k=k):
-                term(i, k, 0).wait_recv()
+                term(i, k, 0, x_right).wait_recv()
 
     gk_ref[0] = (kts[1].astype(F32) + ktr[0].astype(F32) + ktr[1].astype(F32)).astype(BF16)
     gv_ref[0] = (vts[1].astype(F32) + vtr[0].astype(F32) + vtr[1].astype(F32)).astype(BF16)
@@ -495,12 +564,14 @@
     for d in range(1, 4):
         wx(d).wait_send()
         ycopy(0, d, u_piece(d), ubuf, y).wait_send()
-        ycopy(1, d, gsend.at[(y + d) % 4], grecv, y).wait_send()
-        ycopy(2, d, a_piece(d), abuf, y).wait_send()
-        ycopy(3, d, psend.at[(y + d) % 4], precv, y).wait_send()
+        for i in range(CHUNKS):
+            a_copy(i, d, y).wait_send()
+            g_copy(i, d, y).wait_send()
+        ycopy(1, d, psend.at[(y + d) % 4], precv, y).wait_send()
         x_copy(d).wait_send()
-    to_sib.wait_send()
-    d_copy.wait_send()
+    for i in range(CHUNKS):
+        d_copy(i).wait_send()
+        wd_copy(i, c).wait_send()
     for d in range(1, 8):
         z_copy(d).wait_send()
     for i in range(CHUNKS):
@@ -508,13 +579,13 @@
 
             @pl.when(has_left)
             def _(i=i, k=k):
-                halo(i, k, 0).wait_send()
-                term(i, k, 0).wait_send()
+                halo(i, k, 0, x_left).wait_send()
+                term(i, k, 0, x).wait_send()
 
             @pl.when(has_right)
             def _(i=i, k=k):
-                halo(i, k, 1).wait_send()
-                term(i, k, 1).wait_send()
+                halo(i, k, 1, x_right).wait_send()
+                term(i, k, 1, x).wait_send()
 
     for zhigh in range(2):
         for dy in range(4):
@@ -552,10 +623,10 @@
             vmem((3, PATCH, WIDTH), BF16),
             vmem((2, PATCH, WIDTH), BF16),
             vmem((2, PATCH, WIDTH), BF16),
-            vmem((8, 2, 64, HALF), F32),
-            vmem((8, 64, HALF), BF16),
-            vmem((8, 64, HALF), BF16),
-            vmem((8, 64, HALF), BF16),
+            vmem((CHUNKS, 2, 2, 64, HALF), F32),
+            vmem((CHUNKS, 2, 64, HALF), BF16),
+            vmem((CHUNKS, 2, 64, HALF), BF16),
+            vmem((3, 2, 64, HALF), BF16),
             vmem((3, 2, 64, HALF), BF16),
             vmem((2, 64, HALF), BF16),
             vmem((7, 16, HALF), BF16),
@@ -564,14 +635,20 @@
             dma((5,)),
             dma((4 * CHUNKS,)),
             dma((4 * CHUNKS,)),
-            dma((4, 3)),
-            dma((4, 3)),
-            dma((7,)),
-            dma((7,)),
+            dma((2, 3)),
+            dma((2, 3)),
+            dma((CHUNKS, 3)),
+            dma((CHUNKS, 3)),
+            dma((CHUNKS, 3)),
+            dma((CHUNKS, 3)),
+            dma((CHUNKS,)),
+            dma((CHUNKS,)),
+            dma((6,)),
+            dma((6,)),
             dma((4 * CHUNKS,)),
             dma((4 * CHUNKS,)),
-            dma((11,)),
-            dma((11,)),
+            dma((14,)),
+            dma((14,)),
             dma((8,)),
             dma((8,)),
         ],

time: 115 us -> 99.4 us (0.86)
  Pallas kernels: 106 us -> 91.7 us
    pallas_call x1, Pallas kernels: 106 us -> 91.7 us  [per_device(): pl.pallas_call(functools.partial(kernel, factor), out_shape=(rows, rows,...]
where the time goes in v2:
time: 99.4 us; the launch traced here: 98.7 us
  Pallas kernels  91.7 us (92%)
  local copies, waits for them, and re-layouts  6.42 us (6%)
    pallas_call x1, Pallas kernels, per_device(): pl.pallas_call(functools.partial(kernel, factor), out_shape=(rows, rows,...  91.7 us
    unnamed x13, local copies, waits for them, and re-layouts  6.42 us

profile of v2, /device:TPU:90, one launch (start us, length us, event | category | flops | bytes accessed | tf_op | source)
XLA Modules:
  0.0 98.7 jit_solution(6348759042409039047)
XLA Ops:
  0.6 91.7 %mesh_attention.1 = (bf16[1,128,2048]{2,1,0:T(8,128)(2,1)}, bf16[1,128,2048]{2,1,0:T(8,128)(2,1)}, bf16[1,128,2048]{2,1,0:T(8,128)(2,1)}, bf16[1,128,2048]{2,1,0:T(8,128)(2,1)}, f32[64,2048]{1,0:T(8,128)}) custom-call(s32[1,1,2]{2,1,0:T(1,128)} %ids_ref.1, bf16[1,128,2048]{2,1,0:T(8,128)(2,1)} %q_hbm.1, bf16[1,128,2048]{2,1,0:T(8,128)(2,1)} %k_hbm.1, ...), custom_call_target="tpu_custom_call" | custom-call | flops 5000000000 | bytes 6000000 | tf_op jit(solution)/shard_map/mesh_attention/pallas_call | solution.py:603
  92.3 0.0 copy-start.3
  92.3 1.9 %copy.16 = bf16[1,128,2048]{2,1,0:T(8,128)(2,1)} copy(bf16[1,128,2048]{2,1,0:T(8,128)(2,1)} %get-tuple-element.10) | data formatting | bytes 1048576
  94.3 0.0 copy-done.3
  94.3 0.0 copy-start.2
  94.3 0.8 copy.17
  95.1 0.4 copy-done.2
  95.5 0.0 copy-start.1
  95.5 0.8 copy.18
  96.3 0.4 copy-done.1
  96.7 0.0 copy-start
  96.7 0.8 copy.19
  97.5 0.4 copy-done
  97.9 0.8 copy.20
Async XLA Ops:
  92.3 2.0 %copy-start.3 = (bf16[1,128,2048]{2,1,0:T(8,128)(2,1)S(1)}, bf16[1,128,2048]{2,1,0:T(8,128)(2,1)}, u32[]{:S(2)}) copy-start(bf16[1,128,2048]{2,1,0:T(8,128)(2,1)} %get-tuple-element.11) | copy-start | bytes 1572868
  94.3 1.2 %copy-start.2 = (bf16[1,128,2048]{2,1,0:T(8,128)(2,1)S(1)}, bf16[1,128,2048]{2,1,0:T(8,128)(2,1)}, u32[]{:S(2)}) copy-start(bf16[1,128,2048]{2,1,0:T(8,128)(2,1)} %get-tuple-element.12) | copy-start | bytes 1572868
  95.5 1.2 %copy-start.1 = (bf16[1,128,2048]{2,1,0:T(8,128)(2,1)S(1)}, bf16[1,128,2048]{2,1,0:T(8,128)(2,1)}, u32[]{:S(2)}) copy-start(bf16[1,128,2048]{2,1,0:T(8,128)(2,1)} %get-tuple-element.13) | copy-start | bytes 1572868
  96.7 1.2 %copy-start = (f32[64,2048]{1,0:T(8,128)S(1)}, f32[64,2048]{1,0:T(8,128)}, u32[]{:S(2)}) copy-start(f32[64,2048]{1,0:T(8,128)} %get-tuple-element.14) | copy-start | bytes 1572868

commit v3 on v2

--- a/solution.py
+++ b/solution.py
@@ -441,21 +441,20 @@
     tile_ready(1)
     forward(1)
     upstream_part(1)
-    backward(0)
+    gradient(0)
     tile_ready(2)
     forward(2)
     upstream_part(2)
-    gradient(0)
-    backward(1)
+    gradient(1)
     tile_ready(3)
     forward(3)
     upstream_part(3)
-    gradient(1)
+    over_x(1)
     gradient(2)
-    over_x(1)
-    backward(2)
+    backward(0)
+    over_x(2)
     gradient(3)
-    over_x(2)
+    backward(1)
     over_x(3)
 
     nodes_a = abuf[...].reshape(4 * PATCH, HALF)
@@ -467,7 +466,7 @@
         ycopy(1, d, psend.at[(y + d) % 4], precv, y).start()
     precv[y] = psend[y]
 
-    backward(3)
+    backward(2)
 
     d_copy(0).wait_recv()
     own = gw[0, :, c] + dr[0].astype(F32)
@@ -487,6 +486,8 @@
 
     for d in (4, 3, 5, 2, 6, 1, 7):
         z_copy(d).start()
+
+    backward(3)
 
     quarter = zh * 2 + par
     mine = zs[zz, pl.ds(pl.multiple_of(quarter * 16, 16), 16)].astype(F32)
@@ -593,6 +594,19 @@
             @pl.when(jnp.logical_not(spread_same(zhigh, dy)))
             def _(zhigh=zhigh, dy=dy):
                 spread(zhigh, dy, zhigh * 4 + dy).wait_send()
+
+
+def place(*refs):
+    sources, targets, staged, sems = refs[:5], refs[5:10], refs[10:15], refs[15]
+    reads = [pltpu.make_async_copy(sources[i], staged[i], sems.at[0, i]) for i in range(5)]
+    writes = [pltpu.make_async_copy(staged[i], targets[i], sems.at[1, i]) for i in range(5)]
+    for copy in reads:
+        copy.start()
+    for read, write in zip(reads, writes):
+        read.wait()
+        write.start()
+    for copy in writes:
+        copy.wait()
 
 
 def per_device(queries, key_vectors, value_vectors, neighbor_ids, upstream, w_out):
@@ -658,7 +672,15 @@
         cost_estimate=pl.CostEstimate(flops=5_000_000_000, bytes_accessed=6_000_000, transcendentals=800_000),
         name="mesh_attention",
     )(neighbor_ids, queries, key_vectors, value_vectors, upstream, w_out)
-    return tuple(out)
+    anywhere = pl.BlockSpec(memory_space=pl.ANY)
+    return pl.pallas_call(
+        place,
+        out_shape=[jax.ShapeDtypeStruct(o.shape, o.dtype) for o in out],
+        in_specs=[anywhere] * 5,
+        out_specs=[anywhere] * 5,
+        scratch_shapes=[vmem(o.shape, o.dtype) for o in out] + [dma((2, 5))],
+        name="place",
+    )(*out)
 
 
 def solution(mesh):

time: 99.4 us -> 96.1 us (0.967)
  local copies, waits for them, and re-layouts: 6.42 us -> 0 us
  Pallas kernels: 91.7 us -> 95.3 us
    unnamed x13 -> x0, local copies, waits for them, and re-layouts: 6.42 us -> none
    pallas_call x0 -> x1, Pallas kernels: none -> 2.61 us  [per_device(): pl.pallas_call(place, out_shape=[jax.ShapeDtypeStruct(o.shape, o.dtype) f...]
    pallas_call x1, Pallas kernels: 91.7 us -> 92.7 us  [per_device(): pl.pallas_call(functools.partial(kernel, factor), out_shape=(rows, rows,...]
where the time goes in v3:
time: 96.1 us; the launch traced here: 95.9 us
  Pallas kernels  95.3 us (99%)
    pallas_call x1, Pallas kernels, per_device(): pl.pallas_call(functools.partial(kernel, factor), out_shape=(rows, rows,...  92.7 us
    pallas_call x1, Pallas kernels, per_device(): pl.pallas_call(place, out_shape=[jax.ShapeDtypeStruct(o.shape, o.dtype) f...  2.61 us

profile of v3, /device:TPU:90, one launch (start us, length us, event | category | flops | bytes accessed | tf_op | source)
XLA Modules:
  0.0 95.9 jit_solution(7604796524693197941)
XLA Ops:
  0.6 92.7 %mesh_attention.1 = (bf16[1,128,2048]{2,1,0:T(8,128)(2,1)}, bf16[1,128,2048]{2,1,0:T(8,128)(2,1)}, bf16[1,128,2048]{2,1,0:T(8,128)(2,1)}, bf16[1,128,2048]{2,1,0:T(8,128)(2,1)}, f32[64,2048]{1,0:T(8,128)}) custom-call(s32[1,1,2]{2,1,0:T(1,128)} %ids_ref.1, bf16[1,128,2048]{2,1,0:T(8,128)(2,1)} %q_hbm.1, bf16[1,128,2048]{2,1,0:T(8,128)(2,1)} %k_hbm.1, ...), custom_call_target="tpu_custom_call" | custom-call | flops 5000000000 | bytes 6000000 | tf_op jit(solution)/shard_map/mesh_attention/pallas_call | solution.py:617
  93.3 2.6 %place.1 = (bf16[1,128,2048]{2,1,0:T(8,128)(2,1)}, bf16[1,128,2048]{2,1,0:T(8,128)(2,1)}, bf16[1,128,2048]{2,1,0:T(8,128)(2,1)}, bf16[1,128,2048]{2,1,0:T(8,128)(2,1)}, f32[64,2048]{1,0:T(8,128)}) custom-call(bf16[1,128,2048]{2,1,0:T(8,128)(2,1)} %get-tuple-element.10.refs_0_, bf16[1,128,2048]{2,1,0:T(8,128)(2,1)} %get-tuple-element.11.refs_1_, ...), custom_call_target="tpu_custom_call" | custom-call | tf_op jit(solution)/shard_map/place/pallas_call | solution.py:676
